TPU v7x, 32 devices: a whole 2x2x4 slice. The times are simulated.
32 devices in a mesh: dp: 4 (over y, x), ctx: 8 (over z, core).
Axes of the slice: x: 2, y: 2, z: 4, core: 2. Of those that a mesh axis runs over, the one named last changes fastest.
Arguments:
- queries: bfloat16 [4, 1024, 1280], P('dp', 'ctx'), may hold values from -16 to 16
- keys: bfloat16 [4, 1024, 1280], P('dp', 'ctx'), may hold values from -16 to 16
- values: bfloat16 [4, 1024, 1280], P('dp', 'ctx'), may hold values from -6 to 6
- seg_lengths: int32 [4, 8], P('dp'), may hold values from 1 to 768, 1024 in all within a row
- out_grad: bfloat16 [4, 1024, 2560], P('dp', 'ctx'), may hold values from -6 to 6
- w_out: bfloat16 [1280, 2560], P('dp'), may hold values from -0.15625 to 0.15625
Outputs:
- attended: bfloat16 [4, 1024, 2560], P('dp', 'ctx')
- query_grad: bfloat16 [4, 1024, 1280], P('dp', 'ctx')
- key_grad: bfloat16 [4, 1024, 1280], P('dp', 'ctx')
- value_grad: bfloat16 [4, 1024, 1280], P('dp', 'ctx')
- w_out_grad: float32 [1280, 2560], P('dp')
Inputs may be any that keep to these rules, and one draw needn't show every extreme that they name: `seg_lengths`: each record's lengths sum to 1024; the longest of each record is exactly 768.
All inputs are finite; a program needn't handle non-finite values.
Results may differ from a plain program's by a relative error of at most 0.027.
Values may be sent and summed in bfloat16 or wider, within the bound.
A program may use at most 192 MiB of HBM per device.

v0:
```python
import functools
import math

import jax
import jax.numpy as jnp
from jax import lax
from jax.experimental import pallas as pl
from jax.experimental.pallas import tpu as pltpu
from jax.sharding import PartitionSpec as P

HEADS = 10
HD = 128
MASKED_SCORE = -1e30
MESH = pl.DeviceIdType.MESH
BF16 = jnp.bfloat16
F32 = jnp.float32
VMEM_BYTES = 56 * 1024 * 1024


def owner_of(head, n):
    slot, place = divmod(head, n)
    if slot and 2 * place + 2 < n:
        place = 2 * place + 2
    return place, slot


def head_in_slot(me, slot, n):
    if slot == 0:
        return me, me < HEADS
    head, valid = 0, False
    for h in range(slot * n, min(HEADS, (slot + 1) * n)):
        place = owner_of(h, n)[0]
        head = jnp.where(me == place, h, head)
        valid = jnp.logical_or(valid, me == place)
    return head, valid


def dot_nt(a, b):
    return lax.dot_general(a, b, (((1,), (1,)), ((), ())), preferred_element_type=F32)


def dot_tn(a, b):
    return lax.dot_general(a, b, (((0,), (0,)), ((), ())), preferred_element_type=F32)


def dot_nn(a, b):
    return jnp.dot(a, b, preferred_element_type=F32)


def remote(src, dst, send, recv, dp, ctx):
    return pltpu.make_async_remote_copy(
        src_ref=src, dst_ref=dst, send_sem=send, recv_sem=recv, device_id=(dp, ctx), device_id_type=MESH
    )


def greet(n, ndp):
    me, dp = lax.axis_index("ctx"), lax.axis_index("dp")
    barrier = pltpu.get_barrier_semaphore()
    for step in range(1, n):
        pl.semaphore_signal(barrier, inc=1, device_id=(dp, lax.rem(me + step, n)), device_id_type=MESH)
    for step in range(1, ndp):
        pl.semaphore_signal(barrier, inc=1, device_id=(lax.rem(dp + step, ndp), me), device_id_type=MESH)
    pl.semaphore_wait(barrier, n - 1 + ndp - 1)


def whole_kernel(
    n, ndp, parts, block,
    q_ref, k_ref, v_ref, og_ref, w_ref, seg_col_ref, seg_row_ref,
    attended_ref, qg_ref, kg_ref, vg_ref, wg_ref,
    heads_ref, full_ref, grad_ref, result_ref, norm_ref, key_sum, value_sum,
    att_ref, att_t, xsend_buf, xrecv_buf, csum, rbuf, hsum, zbuf, final,
    send_sem, recv_sem, wsend, wrecv, gsend, grecv,
    hsend, hrecv, xsend, xrecv, rsend, rrecv, zsend, zrecv, bsend, brecv, fsend, frecv,
):
    me, dp = lax.axis_index("ctx"), lax.axis_index("dp")
    core = lax.rem(me, 2)
    chip = me // 2
    chips = n // 2
    sibling = me + 1 - 2 * core
    slots, _, seq, _ = heads_ref.shape
    rows = q_ref.shape[0]
    width = og_ref.shape[1]
    wrows = w_ref.shape[0]
    half = wrows // 2
    wide = width // parts
    scale = 1.0 / math.sqrt(HD)
    my_rows = pl.ds(pl.multiple_of(me * rows, rows), rows)
    greet(n, ndp)

    def weight_rows(owner, which):
        return pl.ds(pl.multiple_of(owner * wrows + which * half, 16), half)

    weight_copies = []
    for step in range(1, ndp):
        copy = remote(
            w_ref.at[pl.ds(pl.multiple_of(core * half, 16), half)],
            full_ref.at[weight_rows(dp, core)],
            wsend.at[step], wrecv.at[step], lax.rem(dp + step, ndp), me,
        )
        copy.start()
        weight_copies.append(copy)

    def send_head(tensor, source, head, start):
        place, slot = owner_of(head, n)
        columns = pl.ds(head * HD, HD)
        copy = remote(
            source.at[:, columns], heads_ref.at[slot, tensor, my_rows],
            send_sem.at[tensor, head], recv_sem.at[slot, tensor], dp, place,
        )

        @pl.when(me != place)
        def _():
            if start:
                copy.start()
            else:
                copy.wait_send()

        if start:
            @pl.when(me == place)
            def _():
                heads_ref[slot, tensor, my_rows, :] = source[:, columns]

    def await_head(slot, tensor):
        waited = heads_ref.at[slot, tensor, pl.ds(0, rows * (n - 1))]
        pltpu.make_async_copy(waited, waited, recv_sem.at[slot, tensor]).wait()

    targets = (att_ref, qg_ref, kg_ref, vg_ref)

    def home_copy(slot, tensor, step):
        head, _ = head_in_slot(me, slot, n)
        other = lax.rem(me + step, n)
        columns = pl.ds(pl.multiple_of(head * HD, HD), HD)
        source = result_ref.at[slot, tensor, pl.ds(pl.multiple_of(other * rows, rows), rows)]
        return remote(
            source, targets[tensor].at[:, columns],
            hsend.at[tensor, slot, step], hrecv.at[tensor, head], dp, other,
        )

    def send_home(slot, tensor):
        head, _ = head_in_slot(me, slot, n)
        for step in range(1, n):
            home_copy(slot, tensor, step).start()
        columns = pl.ds(pl.multiple_of(head * HD, HD), HD)
        targets[tensor][:, columns] = result_ref[slot, tensor, my_rows, :]

    def receive_home(tensor):
        for head in range(HEADS):
            place, _ = owner_of(head, n)

            @pl.when(me != place)
            def _():
                landed = targets[tensor].at[:, pl.ds(head * HD, HD)]
                remote(landed, landed, hsend.at[tensor, 0, 0], hrecv.at[tensor, head], dp, place).wait_recv()

    for tensor, source in enumerate((q_ref, k_ref, v_ref)):
        for head in range(HEADS):
            send_head(tensor, source, head, True)
    full_ref[pl.ds(pl.multiple_of(dp * wrows, 16), wrows), :] = w_ref[...]

    def block_scores(slot, span):
        seen = seg_col_ref[span, :] == seg_row_ref[...]
        scores = dot_nt(heads_ref[slot, 0, span, :], heads_ref[slot, 1]) * scale
        return jnp.where(seen, scores, MASKED_SCORE)

    for slot in range(slots):
        @pl.when(head_in_slot(me, slot, n)[1])
        def _():
            for tensor in range(3):
                await_head(slot, tensor)

            @pl.loop(0, seq // block)
            def _(index):
                span = pl.ds(pl.multiple_of(index * block, block), block)
                scores = block_scores(slot, span)
                top = jnp.max(scores, axis=1, keepdims=True)
                shifted = jnp.exp(scores - top)
                total = jnp.sum(shifted, axis=1, keepdims=True)
                norm_ref[slot, span, :] = top + jnp.log(total)
                probs_b = (shifted * (1.0 / total)).astype(BF16)
                result_ref[slot, 0, span, :] = dot_nn(probs_b, heads_ref[slot, 2]).astype(BF16)

            send_home(slot, 0)

    passes = []
    for step in range(1, ndp):
        weight_copies[step - 1].wait_recv()
        source = lax.rem(dp - step + ndp, ndp)
        landed = full_ref.at[weight_rows(source, core)]
        copy = remote(landed, landed, gsend.at[step], grecv.at[step], dp, sibling)
        copy.start()
        passes.append(copy)
    for copy in passes:
        copy.wait_recv()
    for head in range(HEADS):
        columns = pl.ds(head * HD, HD)
        grad_ref[:, columns] = dot_nt(og_ref[...], full_ref[columns, :]).astype(BF16)
        send_head(3, grad_ref, head, True)

    receive_home(0)
    att_t[...] = att_ref[...].T

    def share(owner, which):
        return pl.multiple_of(owner * 2 * half + which * half, 16)

    def part_columns(part):
        return pl.ds(part * wide, wide)

    def owner_at(step):
        return lax.rem(dp + step + 1, ndp)

    def pair_copy(part, step):
        columns = part_columns(part)
        return remote(
            xsend_buf.at[step, :, columns], xrecv_buf.at[step, :, columns],
            xsend.at[step, part], xrecv.at[step, part], dp, sibling,
        )

    def dp_copy(part, step):
        columns = part_columns(part)
        return remote(
            csum.at[step, :, columns], rbuf.at[step, :, columns],
            rsend.at[step, part], rrecv.at[step, part], owner_at(step), me,
        )

    for part in range(parts):
        columns = part_columns(part)
        for step in range(ndp):
            left = att_t[pl.ds(share(owner_at(step), 1 - core), half), :]
            xsend_buf[step, :, columns] = dot_nn(left, og_ref[:, columns]).astype(BF16)
            pair_copy(part, step).start()
    for part in range(parts):
        columns = part_columns(part)
        for step in range(ndp):
            left = att_t[pl.ds(share(owner_at(step), core), half), :]
            mine = dot_nn(left, og_ref[:, columns])
            pair_copy(part, step).wait_recv()
            csum[step, :, columns] = (mine + xrecv_buf[step, :, columns].astype(F32)).astype(BF16)
            if step < ndp - 1:
                dp_copy(part, step).start()

    for slot in range(slots):
        @pl.when(head_in_slot(me, slot, n)[1])
        def _():
            await_head(slot, 3)
            key_sum[...] = jnp.zeros_like(key_sum)
            value_sum[...] = jnp.zeros_like(value_sum)

            @pl.loop(0, seq // block)
            def _(index):
                span = pl.ds(pl.multiple_of(index * block, block), block)
                grad = heads_ref[slot, 3, span, :]
                probs = jnp.exp(block_scores(slot, span) - norm_ref[slot, span, :])
                attention = result_ref[slot, 0, span, :]
                grad_dot = jnp.sum(grad.astype(F32) * attention.astype(F32), axis=1, keepdims=True)
                dscore = (probs * (dot_nt(grad, heads_ref[slot, 2]) - grad_dot)).astype(BF16)
                result_ref[slot, 1, span, :] = (dot_nn(dscore, heads_ref[slot, 1]) * scale).astype(BF16)
                key_sum[...] += dot_tn(dscore, heads_ref[slot, 0, span, :])
                value_sum[...] += dot_tn(probs.astype(BF16), grad)

            result_ref[slot, 2] = (key_sum[...] * scale).astype(BF16)
            result_ref[slot, 3] = value_sum[...].astype(BF16)
            for tensor in range(1, 4):
                send_home(slot, tensor)

    @pl.loop(0, width // 512)
    def _(index):
        columns = pl.ds(pl.multiple_of(index * 512, 512), 512)
        attended_ref[:, columns] = dot_nn(att_ref[...], full_ref[:, columns]).astype(BF16)

    my_half = pl.ds(pl.multiple_of(core * half, 16), half)
    their_half = pl.ds(pl.multiple_of((1 - core) * half, 16), half)

    def sum_copy(part):
        return remote(
            hsum.at[:, part_columns(part)], zbuf.at[chip],
            zsend.at[part], zrecv.at[chip], dp, 2 * part + core,
        )

    def spread_copy(part, other):
        landed = final.at[my_half, part_columns(part)]
        return remote(landed, landed, bsend.at[other], brecv.at[part], dp, 2 * other + core)

    def pass_copy(part, span):
        landed = final.at[span, part_columns(part)]
        return remote(landed, landed, fsend.at[part], frecv.at[part], dp, sibling)

    def finish(part):
        @pl.when(chip == part)
        def _():
            total = hsum[:, part_columns(part)].astype(F32)
            for other in range(chips):
                if other != part:
                    landed = zbuf.at[other]
                    remote(landed, landed, zsend.at[0], zrecv.at[other], dp, 2 * other + core).wait_recv()
                    total = total + zbuf[other].astype(F32)
            final[my_half, part_columns(part)] = total.astype(BF16)
            for other in range(chips):
                if other != part:
                    spread_copy(part, other).start()

    for part in range(parts):
        columns = part_columns(part)
        total = csum[ndp - 1, :, columns].astype(F32)
        for step in range(ndp - 1):
            dp_copy(part, step).wait_recv()
            total = total + rbuf[step, :, columns].astype(F32)
        hsum[:, columns] = total.astype(BF16)

        @pl.when(chip != part)
        def _():
            sum_copy(part).start()

        if part:
            finish(part - 1)
    finish(parts - 1)

    for part in range(parts):
        @pl.when(chip != part)
        def _():
            spread_copy(part, part).wait_recv()

        pass_copy(part, my_half).start()
    for part in range(parts):
        pass_copy(part, their_half).wait_recv()
    wg_ref[...] = final[...]

    for tensor in range(1, 4):
        receive_home(tensor)
    for tensor, source in enumerate((q_ref, k_ref, v_ref, grad_ref)):
        for head in range(HEADS):
            send_head(tensor, source, head, False)
    for copy in weight_copies + passes:
        copy.wait_send()
    for slot in range(slots):
        @pl.when(head_in_slot(me, slot, n)[1])
        def _():
            for tensor in range(4):
                for step in range(1, n):
                    home_copy(slot, tensor, step).wait_send()
    for part in range(parts):
        for step in range(ndp):
            pair_copy(part, step).wait_send()
            if step < ndp - 1:
                dp_copy(part, step).wait_send()
        pass_copy(part, my_half).wait_send()

        @pl.when(chip != part)
        def _():
            sum_copy(part).wait_send()

        @pl.when(chip == part)
        def _():
            for other in range(chips):
                if other != part:
                    spread_copy(part, other).wait_send()


def copy_kernel(*refs):
    sources, targets, held = refs[:5], refs[5:10], refs[10:15]
    wide_held, in_sem, out_sem = refs[15:]
    loads = [pltpu.make_async_copy(sources[i], held[i], in_sem.at[i]) for i in range(5)]
    stores = [
        pltpu.make_async_copy(held[i] if i < 4 else wide_held, targets[i], out_sem.at[i]) for i in range(5)
    ]
    for i in (4, 0, 1, 2, 3):
        loads[i].start()
    loads[4].wait()
    wide_held[...] = held[4][...].astype(F32)
    stores[4].start()
    for i in range(4):
        loads[i].wait()
        stores[i].start()
    for store in stores:
        store.wait()


def segment_ids(length_row, row_total):
    order = lax.iota(jnp.int32, length_row.shape[0])
    segment_ends = jnp.sum(jnp.where(order[None, :] <= order[:, None], length_row[None, :], 0), axis=1)
    positions = lax.iota(jnp.int32, row_total)
    return jnp.sum((segment_ends[None, :] <= positions[:, None]).astype(jnp.int32), axis=1)


def vmem(count):
    return [pl.BlockSpec(memory_space=pltpu.VMEM)] * count


def local(queries, keys, values, seg_lengths, out_grad, w_out):
    n, ndp = lax.axis_size("ctx"), lax.axis_size("dp")
    rows, inner = queries.shape[1:]
    width = out_grad.shape[2]
    seq = rows * n
    wrows = w_out.shape[0]
    half = wrows // 2
    slots = -(-HEADS // n)
    parts = math.gcd(n // 2, width // 128)
    wide = width // parts
    shape = jax.ShapeDtypeStruct
    dma = pltpu.SemaphoreType.DMA
    segments = segment_ids(seg_lengths[0], seq)
    out_shape = (
        shape((rows, width), BF16), shape((rows, inner), BF16), shape((rows, inner), BF16),
        shape((rows, inner), BF16), shape((wrows, width), F32),
    )
    outputs = pl.pallas_call(
        functools.partial(whole_kernel, n, ndp, parts, 256),
        out_shape=out_shape[:4] + (shape((wrows, width), BF16),),
        in_specs=vmem(7),
        out_specs=tuple(vmem(5)),
        scratch_shapes=[
            pltpu.VMEM((slots, 4, seq, HD), BF16),
            pltpu.VMEM((inner, width), BF16),
            pltpu.VMEM((rows, inner), BF16),
            pltpu.VMEM((slots, 4, seq, HD), BF16),
            pltpu.VMEM((slots, seq, 1), F32),
            pltpu.VMEM((seq, HD), F32),
            pltpu.VMEM((seq, HD), F32),
            pltpu.VMEM((rows, inner), BF16),
            pltpu.VMEM((inner, rows), BF16),
            pltpu.VMEM((ndp, half, width), BF16),
            pltpu.VMEM((ndp, half, width), BF16),
            pltpu.VMEM((ndp, half, width), BF16),
            pltpu.VMEM((ndp - 1, half, width), BF16),
            pltpu.VMEM((half, width), BF16),
            pltpu.VMEM((n // 2, half, wide), BF16),
            pltpu.VMEM((wrows, width), BF16),
            dma((4, HEADS)), dma((slots, 4)), dma((ndp,)), dma((ndp,)), dma((ndp,)), dma((ndp,)),
            dma((4, slots, n)), dma((4, HEADS)),
            dma((ndp, parts)), dma((ndp, parts)), dma((ndp, parts)), dma((ndp, parts)),
            dma((parts,)), dma((n // 2,)), dma((n // 2,)), dma((parts,)), dma((parts,)), dma((parts,)),
        ],
        compiler_params=pltpu.CompilerParams(
            collective_id=0, has_side_effects=True, vmem_limit_bytes=VMEM_BYTES
        ),
    )(queries[0], keys[0], values[0], out_grad[0], w_out, segments[:, None], segments[None, :])
    anywhere = [pl.BlockSpec(memory_space=pl.ANY)] * 5
    attended, query_grad, key_grad, value_grad, weight_grad = pl.pallas_call(
        copy_kernel,
        out_shape=out_shape,
        in_specs=anywhere,
        out_specs=tuple(anywhere),
        scratch_shapes=[pltpu.VMEM(x.shape, BF16) for x in out_shape]
        + [pltpu.VMEM((wrows, width), F32), dma((5,)), dma((5,))],
        compiler_params=pltpu.CompilerParams(vmem_limit_bytes=VMEM_BYTES),
    )(*outputs)
    return (attended[None], query_grad[None], key_grad[None], value_grad[None], weight_grad)


def solution(mesh):
    in_specs = (
        P("dp", "ctx", None),
        P("dp", "ctx", None),
        P("dp", "ctx", None),
        P("dp", None),
        P("dp", "ctx", None),
        P("dp", None),
    )
    out_specs = (
        P("dp", "ctx", None),
        P("dp", "ctx", None),
        P("dp", "ctx", None),
        P("dp", "ctx", None),
        P("dp", None),
    )
    return jax.shard_map(local, mesh=mesh, in_specs=in_specs, out_specs=out_specs, check_vma=False)
```

profile of v0, /device:TPU:17, one launch (start us, length us, event | category | flops | bytes accessed | tf_op | source)
XLA Modules:
  0.0 155.9 jit_solution(5235571205312527343)
XLA Ops:
  0.6 0.8 select_reduce_fusion
  1.4 0.1 convert_reduce_fusion
  1.5 0.0 copy-start
  1.5 1.0 copy.12.seg_col_ref
  2.5 0.0 copy-done
  2.5 149.4 %shard_map.101 = (bf16[128,2560]{1,0:T(8,128)(2,1)}, bf16[128,1280]{1,0:T(8,128)(2,1)}, bf16[128,1280]{1,0:T(8,128)(2,1)}, bf16[128,1280]{1,0:T(8,128)(2,1)}, bf16[320,2560]{1,0:T(8,128)(2,1)}) custom-call(bf16[128,1280]{1,0:T(8,128)(2,1)} %bitcast.12, bf16[128,1280]{1,0:T(8,128)(2,1)} %bitcast.13, bf16[128,1280]{1,0:T(8,128)(2,1)} %bitcast.14, ...), custom_call_target="tpu_custom_call" | custom-call | tf_op jit(solution)/shard_map/pallas_call | solution.py:405
  152.0 4.0 %shard_map.102 = (bf16[128,2560]{1,0:T(8,128)(2,1)}, bf16[128,1280]{1,0:T(8,128)(2,1)}, bf16[128,1280]{1,0:T(8,128)(2,1)}, bf16[128,1280]{1,0:T(8,128)(2,1)}, f32[320,2560]{1,0:T(8,128)}) custom-call(bf16[128,2560]{1,0:T(8,128)(2,1)} %get-tuple-element.15.refs_0_, bf16[128,1280]{1,0:T(8,128)(2,1)} %get-tuple-element.16.refs_1_, ...), custom_call_target="tpu_custom_call" | custom-call | tf_op jit(solution)/shard_map/pallas_call | solution.py:437
Async XLA Ops:
  1.5 1.0 copy-start
where the time goes:
time: 156 us
  Pallas kernels  153 us (98%)
    pallas_call x1, Pallas kernels, local(): pl.pallas_call(functools.partial(whole_kernel, n, ndp, parts, 256), out_s...  149 us
    pallas_call x1, Pallas kernels, local(): pl.pallas_call(copy_kernel, out_shape=out_shape, in_specs=anywhere, out_s...  3.96 us

commit v1 on v0

v1 whole, which is shorter than its diff:
```python
import functools
import math

import jax
import jax.numpy as jnp
from jax import lax
from jax.experimental import pallas as pl
from jax.experimental.pallas import tpu as pltpu
from jax.sharding import PartitionSpec as P

HEADS = 10
HD = 128
MASKED_SCORE = -1e30
MESH = pl.DeviceIdType.MESH
BF16 = jnp.bfloat16
F32 = jnp.float32
VMEM_BYTES = 56 * 1024 * 1024


def owner_of(head, n):
    slot, place = divmod(head, n)
    if slot and 2 * place + 2 < n:
        place = 2 * place + 2
    return place, slot


def head_in_slot(me, slot, n):
    if slot == 0:
        return me, me < HEADS
    head, valid = 0, False
    for h in range(slot * n, min(HEADS, (slot + 1) * n)):
        place = owner_of(h, n)[0]
        head = jnp.where(me == place, h, head)
        valid = jnp.logical_or(valid, me == place)
    return head, valid


def dot_nt(a, b):
    return lax.dot_general(a, b, (((1,), (1,)), ((), ())), preferred_element_type=F32)


def dot_tn(a, b):
    return lax.dot_general(a, b, (((0,), (0,)), ((), ())), preferred_element_type=F32)


def dot_nn(a, b):
    return jnp.dot(a, b, preferred_element_type=F32)


def remote(src, dst, send, recv, dp, ctx):
    return pltpu.make_async_remote_copy(
        src_ref=src, dst_ref=dst, send_sem=send, recv_sem=recv, device_id=(dp, ctx), device_id_type=MESH
    )


def greet(n, ndp):
    me, dp = lax.axis_index("ctx"), lax.axis_index("dp")
    barrier = pltpu.get_barrier_semaphore()
    for down in range(ndp):
        for step in range(n):
            if down or step:
                pl.semaphore_signal(
                    barrier, inc=1, device_id=(lax.rem(dp + down, ndp), lax.rem(me + step, n)), device_id_type=MESH
                )
    pl.semaphore_wait(barrier, n * ndp - 1)


def whole_kernel(
    n, ndp, parts, block, span,
    seg_ref, q_ref, k_ref, v_ref, og_ref, w_ref,
    attended_ref, qg_ref, kg_ref, vg_ref, wg_ref,
    heads_ref, result_ref, probs_ref, dscore_ref, turned, query_mask, key_mask,
    w_pad, og_all, att_all, att_t, grad_ref, psend_buf, precv_buf, pown,
    xsend_buf, xrecv_buf, own_sum, chain_buf, outer_buf, middle_buf,
    send_sem, recv_sem, osend, orecv, gsend, grecv, asend, arecv, hsend, hrecv,
    psend, precv, xsend, xrecv, csend, crecv, mrecv, bsend, brecv, fsend, frecv,
):
    me, dp = lax.axis_index("ctx"), lax.axis_index("dp")
    core = lax.rem(me, 2)
    chip = me // 2
    chips = n // 2
    sibling = me + 1 - 2 * core
    slots, _, seq, _ = heads_ref.shape
    rows = q_ref.shape[0]
    width = og_ref.shape[1]
    wrows = w_ref.shape[0]
    half = wrows // 2
    wide = width // parts
    scale = 1.0 / math.sqrt(HD)
    my_rows = pl.ds(pl.multiple_of(me * rows, rows), rows)
    first = dp * wrows // HD
    lead = dp * wrows - first * HD
    greet(n, ndp)

    def record_rows(record):
        return pl.ds(pl.multiple_of(record * rows, rows), rows)

    def head_columns(head):
        if isinstance(head, int):
            return pl.ds(head * HD, HD)
        return pl.ds(pl.multiple_of(head * HD, HD), HD)

    def place_of(head):
        slot = head // n
        place = head - slot * n
        if slots > 1:
            moved = 2 * place + 2
            place = jnp.where(jnp.logical_and(slot > 0, moved < n), moved, place)
        return place, slot

    def low_source(head):
        return head * HD // wrows

    def high_source(head):
        return (head * HD + HD - 1) // wrows

    def send_head(tensor, source, head, start):
        place, slot = owner_of(head, n)
        columns = head_columns(head)
        copy = remote(
            source.at[:, columns], heads_ref.at[slot, tensor, my_rows],
            send_sem.at[tensor, head], recv_sem.at[slot, tensor], dp, place,
        )

        @pl.when(me != place)
        def _():
            if start:
                copy.start()
            else:
                copy.wait_send()

        if start:
            @pl.when(me == place)
            def _():
                heads_ref[slot, tensor, my_rows, :] = source[:, columns]

    def await_head(slot, tensor):
        waited = heads_ref.at[slot, tensor, pl.ds(0, rows * (n - 1))]
        pltpu.make_async_copy(waited, waited, recv_sem.at[slot, tensor]).wait()

    def og_copy(source, at, count, record, sem, slot, peer):
        landed = pl.ds(pl.multiple_of(record * rows + at, 16), count)
        return remote(source, og_all.at[landed], osend.at[sem], orecv.at[slot], peer, me)

    spread = []
    if ndp == 4:
        cut = rows // 2
        across = dp + 1 - 2 * lax.rem(dp, 2)
        along = lax.rem(dp + 2, 4)
        corner = 3 - dp
        peers = (across, along, corner)
        for order in range(2):
            for axis, peer in enumerate((across, along)):
                part = order if axis == 0 else 1 - order
                copy = og_copy(og_ref.at[pl.ds(part * cut, cut)], part * cut, cut, dp, 2 * axis + part, 2 * axis + part, peer)
                copy.start()
                spread.append(copy)
    else:
        peers = tuple(lax.rem(dp + ndp - step, ndp) for step in range(1, ndp))
        for step in range(1, ndp):
            copy = og_copy(og_ref, 0, rows, dp, step, step, lax.rem(dp + step, ndp))
            copy.start()
            spread.append(copy)

    for tensor, source in enumerate((q_ref, k_ref, v_ref)):
        for head in range(HEADS):
            send_head(tensor, source, head, True)

    w_pad[...] = jnp.zeros_like(w_pad)
    w_pad[pl.ds(pl.multiple_of(lead, 16), wrows), :] = w_ref[...]
    og_all[record_rows(dp), :] = og_ref[...]

    def grad_copy(step, record, spot):
        head = first + spot
        place, slot = place_of(head)
        which = dp - low_source(head)
        return remote(
            grad_ref.at[step, :, head_columns(spot)], heads_ref.at[slot, 3 + which, my_rows],
            gsend.at[step, spot], grecv.at[slot, which], record, place,
        )

    def make_grad(step, record):
        grad_ref[step] = dot_nt(og_all[record_rows(record), :], w_pad[...]).astype(BF16)
        for spot in range(span):
            if step:
                grad_copy(step, record, spot).start()
            else:
                place, slot = place_of(first + spot)

                @pl.when(place == me)
                def _():
                    heads_ref[slot, 3 + dp - low_source(first + spot), my_rows, :] = grad_ref[0, :, head_columns(spot)]

                @pl.when(place != me)
                def _():
                    grad_copy(0, record, spot).start()

    make_grad(0, dp)

    @pl.loop(0, seq // block)
    def _(index):
        at = pl.ds(pl.multiple_of(index * block, block), block)
        position = lax.broadcasted_iota(jnp.int32, (block, HD), 0) + index * block
        lane = lax.broadcasted_iota(jnp.int32, (block, HD), 1)
        count = seg_ref.shape[1]
        end = jnp.int32(0)
        segment = jnp.zeros((block, HD), jnp.int32)
        for i in range(count):
            end = end + seg_ref[0, i]
            segment = segment + jnp.where(position >= end, 1, 0)
        query_mask[at, :] = jnp.where(segment == lane, 1.0, 0.0).astype(BF16)
        key_mask[at, :] = jnp.where(jnp.logical_or(segment == lane, lane >= count), 0.0, MASKED_SCORE).astype(BF16)

    def await_og(slot, at, count, record):
        landed = og_all.at[pl.ds(pl.multiple_of(record * rows + at, 16), count)]
        remote(landed, landed, osend.at[0], orecv.at[slot], dp, me).wait_recv()
        return landed

    if ndp == 4:
        for axis, (peer, other) in enumerate(((across, along), (along, across))):
            landed = await_og(3 * axis, axis * cut, cut, peer)
            copy = og_copy(landed, axis * cut, cut, peer, 4 + axis, 4 + axis, other)
            copy.start()
            spread.append(copy)
        for axis, peer in enumerate((across, along)):
            await_og(axis + 1, (1 - axis) * cut, cut, peer)
            make_grad(axis + 1, peer)
        for axis in range(2):
            await_og(4 + axis, axis * cut, cut, corner)
        make_grad(3, corner)
    else:
        for step, peer in enumerate(peers, 1):
            await_og(step, 0, rows, peer)
            make_grad(step, peer)

    def attention_copy(slot, step, which):
        head, _ = head_in_slot(me, slot, n)
        other = lax.rem(me + step, n)
        target = low_source(head) + which
        spot = head - target * wrows // HD
        source = result_ref.at[slot, 0, pl.ds(pl.multiple_of(other * rows, rows), rows)]
        return target, spot, remote(
            source, att_all.at[record_rows(dp), head_columns(spot)],
            asend.at[slot, step, which], arecv.at[dp, spot], target, other,
        )

    def attention_copies(slot, start):
        head, _ = head_in_slot(me, slot, n)
        for which in range(2):
            @pl.when(low_source(head) + which <= high_source(head))
            def _():
                for step in range(n):
                    target, spot, copy = attention_copy(slot, step, which)

                    def act():
                        if start:
                            copy.start()
                        else:
                            copy.wait_send()

                    if step:
                        act()
                    else:
                        pl.when(target != dp)(act)
                        if start:
                            @pl.when(target == dp)
                            def _():
                                att_all[record_rows(dp), head_columns(spot)] = result_ref[slot, 0, my_rows, :]

    log2e = math.log2(math.e)
    for slot in range(slots):
        @pl.when(head_in_slot(me, slot, n)[1])
        def _():
            for tensor in range(3):
                await_head(slot, tensor)
            turned[...] = heads_ref[slot, 2].T

            @pl.loop(0, seq // block)
            def _(index):
                at = pl.ds(pl.multiple_of(index * block, block), block)
                left = jnp.concatenate([heads_ref[slot, 1], key_mask[...]], axis=1)
                right = jnp.concatenate([heads_ref[slot, 0, at, :], query_mask[at, :]], axis=1)
                scores = dot_nt(left, right)
                top = jnp.max(scores, axis=0, keepdims=True)
                shifted = jnp.exp2((scores - top) * (scale * log2e))
                total = jnp.sum(shifted, axis=0, keepdims=True)
                probs_b = (shifted * (1.0 / total)).astype(BF16)
                probs_ref[slot, :, at] = probs_b
                result_ref[slot, 0, at, :] = dot_nn(turned[...], probs_b).astype(BF16).T

            attention_copies(slot, True)

    targets = (None, qg_ref, kg_ref, vg_ref)

    def home_copy(slot, tensor, step):
        head, _ = head_in_slot(me, slot, n)
        other = lax.rem(me + step, n)
        source = result_ref.at[slot, tensor, pl.ds(pl.multiple_of(other * rows, rows), rows)]
        return remote(
            source, targets[tensor].at[:, head_columns(head)],
            hsend.at[tensor, slot, step], hrecv.at[tensor, head], dp, other,
        )

    def send_home(slot, tensor):
        head, _ = head_in_slot(me, slot, n)
        for step in range(1, n):
            home_copy(slot, tensor, step).start()
        targets[tensor][:, head_columns(head)] = result_ref[slot, tensor, my_rows, :]

    def receive_home(tensor):
        for head in range(HEADS):
            place, _ = owner_of(head, n)

            @pl.when(me != place)
            def _():
                landed = targets[tensor].at[:, head_columns(head)]
                remote(landed, landed, hsend.at[tensor, 0, 0], hrecv.at[tensor, head], dp, place).wait_recv()

    for slot in range(slots):
        @pl.when(head_in_slot(me, slot, n)[1])
        def _():
            head, _ = head_in_slot(me, slot, n)
            turned[...] = heads_ref[slot, 1].T
            for which in range(2):
                source = low_source(head) + which

                def await_grad(count):
                    waited = heads_ref.at[slot, 3 + which, pl.ds(0, rows * count)]
                    pltpu.make_async_copy(waited, waited, grecv.at[slot, which]).wait()

                @pl.when(source <= high_source(head))
                def _():
                    pl.when(source == dp)(lambda: await_grad(n - 1))
                    pl.when(source != dp)(lambda: await_grad(n))
                    if which:
                        heads_ref[slot, 3] = heads_ref[slot, 3] + heads_ref[slot, 4]

            @pl.loop(0, seq // block)
            def _(index):
                at = pl.ds(pl.multiple_of(index * block, block), block)
                result_ref[slot, 3, at, :] = dot_nn(probs_ref[slot, at, :], heads_ref[slot, 3]).astype(BF16)

            send_home(slot, 3)

            @pl.loop(0, seq // block)
            def _(index):
                at = pl.ds(pl.multiple_of(index * block, block), block)
                grad = heads_ref[slot, 3, at, :]
                product = grad.astype(F32) * result_ref[slot, 0, at, :].astype(F32)
                grad_dot = jnp.sum(product.T, axis=0, keepdims=True)
                dprob = dot_nt(heads_ref[slot, 2], grad)
                dscore = (probs_ref[slot, :, at].astype(F32) * (dprob - grad_dot)).astype(BF16)
                dscore_ref[:, at] = dscore
                result_ref[slot, 1, at, :] = (dot_nn(turned[...], dscore) * scale).astype(BF16).T

            send_home(slot, 1)

            @pl.loop(0, seq // block)
            def _(index):
                at = pl.ds(pl.multiple_of(index * block, block), block)
                result_ref[slot, 2, at, :] = (dot_nn(dscore_ref[at, :], heads_ref[slot, 0]) * scale).astype(BF16)

            send_home(slot, 2)

    for record in range(ndp):
        for spot in range(span):
            landed = att_all.at[record_rows(record), head_columns(spot)]
            here = jnp.logical_and(record == dp, place_of(first + spot)[0] == me)

            @pl.when(jnp.logical_not(here))
            def _():
                remote(landed, landed, asend.at[0, 0, 0], arecv.at[record, spot], dp, sibling).wait_recv()

    def part_columns(part):
        return pl.ds(part * wide, wide)

    def share(which):
        return pl.ds(pl.multiple_of(lead + which * half, 16), half)

    def pair_copy(part):
        columns = part_columns(part)
        return remote(
            xsend_buf.at[:, columns], xrecv_buf.at[:, columns], xsend.at[part], xrecv.at[part], dp, sibling,
        )

    def partial_copy(part, step):
        columns = part_columns(part)
        other = lax.rem(dp + step, ndp)
        return remote(
            psend_buf.at[record_rows(other), columns], precv_buf.at[step, :, columns],
            psend.at[part, step], precv.at[part, step], other, me,
        )

    att_t[...] = att_all[...].T
    for part in range(parts):
        columns = part_columns(part)
        xsend_buf[:, columns] = dot_nn(att_t[share(1 - core), :], og_all[:, columns]).astype(BF16)
        pair_copy(part).start()
    for part in range(parts):
        columns = part_columns(part)
        psend_buf[:, columns] = dot_nn(att_all[...], w_pad[:, columns]).astype(BF16)
        for step in range(1, ndp):
            partial_copy(part, step).start()

    my_half = pl.ds(pl.multiple_of(core * half, 16), half)
    their_half = pl.ds(pl.multiple_of((1 - core) * half, 16), half)
    depth = jnp.where(chip < chips // 2, chip, chips - 1 - chip)
    toward = jnp.where(chip < chips // 2, 1, -1)
    innermost = depth == chips // 2 - 1
    inner = me + 2 * toward
    outer = me - 2 * toward

    def inward_copy(part):
        columns = part_columns(part)
        return remote(
            chain_buf.at[:, columns], outer_buf.at[:, columns], csend.at[part], crecv.at[part], dp, inner,
        )

    def middle_copy(part):
        columns = part_columns(part)
        return remote(
            chain_buf.at[:, columns], middle_buf.at[:, columns], csend.at[part], mrecv.at[part], dp, inner,
        )

    def outward_copy(part):
        landed = wg_ref.at[my_half, part_columns(part)]
        return remote(landed, landed, bsend.at[part], brecv.at[part], dp, outer)

    def pass_copy(part, held):
        landed = wg_ref.at[held, part_columns(part)]
        return remote(landed, landed, fsend.at[part], frecv.at[part], dp, sibling)

    def finish(part):
        columns = part_columns(part)

        @pl.when(innermost)
        def _():
            middle_copy(part).wait_recv()
            total = chain_buf[:, columns].astype(F32) + middle_buf[:, columns].astype(F32)
            wg_ref[my_half, columns] = total.astype(BF16)

        @pl.when(jnp.logical_not(innermost))
        def _():
            outward_copy(part).wait_recv()

        @pl.when(depth > 0)
        def _():
            outward_copy(part).start()

        pass_copy(part, my_half).start()

    for part in range(parts):
        columns = part_columns(part)
        own_sum[...] = dot_nn(att_t[share(core), :], og_all[:, columns])
        pair_copy(part).wait_recv()
        own_sum[...] += xrecv_buf[:, columns].astype(F32)

        @pl.when(depth > 0)
        def _():
            inward_copy(part).wait_recv()
            own_sum[...] += outer_buf[:, columns].astype(F32)

        chain_buf[:, columns] = own_sum[...].astype(BF16)

        @pl.when(innermost)
        def _():
            middle_copy(part).start()

        @pl.when(jnp.logical_not(innermost))
        def _():
            inward_copy(part).start()

        if part:
            finish(part - 1)
    finish(parts - 1)

    for part in range(parts):
        columns = part_columns(part)
        total = psend_buf[record_rows(dp), columns].astype(F32)
        for step in range(1, ndp):
            partial_copy(part, step).wait_recv()
            total = total + precv_buf[step, :, columns].astype(F32)
        attended_ref[:, columns] = total.astype(BF16)

    for part in range(parts):
        pass_copy(part, their_half).wait_recv()
    for tensor in range(1, 4):
        receive_home(tensor)

    for tensor, source in enumerate((q_ref, k_ref, v_ref)):
        for head in range(HEADS):
            send_head(tensor, source, head, False)
    for copy in spread:
        copy.wait_send()
    for step, record in enumerate((dp,) + peers):
        for spot in range(span):
            copy = grad_copy(step, record, spot)
            if step:
                copy.wait_send()
            else:
                pl.when(place_of(first + spot)[0] != me)(copy.wait_send)
    for slot in range(slots):
        @pl.when(head_in_slot(me, slot, n)[1])
        def _():
            attention_copies(slot, False)
            for tensor in range(1, 4):
                for step in range(1, n):
                    home_copy(slot, tensor, step).wait_send()
    for part in range(parts):
        pair_copy(part).wait_send()
        for step in range(1, ndp):
            partial_copy(part, step).wait_send()
        inward_copy(part).wait_send()
        pl.when(depth > 0)(outward_copy(part).wait_send)
        pass_copy(part, my_half).wait_send()


def copy_kernel(*refs):
    sources, targets, held = refs[:5], refs[5:10], refs[10:15]
    wide_held, in_sem, out_sem = refs[15:]
    loads = [pltpu.make_async_copy(sources[i], held[i], in_sem.at[i]) for i in range(5)]
    stores = [
        pltpu.make_async_copy(held[i] if i < 4 else wide_held, targets[i], out_sem.at[i]) for i in range(5)
    ]
    for i in (4, 0, 1, 2, 3):
        loads[i].start()
    loads[4].wait()
    wide_held[...] = held[4][...].astype(F32)
    stores[4].start()
    for i in range(4):
        loads[i].wait()
        stores[i].start()
    for store in stores:
        store.wait()


def vmem(count):
    return [pl.BlockSpec(memory_space=pltpu.VMEM)] * count


def local(queries, keys, values, seg_lengths, out_grad, w_out):
    n, ndp = lax.axis_size("ctx"), lax.axis_size("dp")
    rows, inner = queries.shape[1:]
    width = out_grad.shape[2]
    seq = rows * n
    wrows = w_out.shape[0]
    half = wrows // 2
    slots = -(-HEADS // n)
    parts = 4
    wide = width // parts
    span = max(-(-(k + 1) * wrows // HD) - k * wrows // HD for k in range(ndp))
    shape = jax.ShapeDtypeStruct
    dma = pltpu.SemaphoreType.DMA
    out_shape = (
        shape((rows, width), BF16), shape((rows, inner), BF16), shape((rows, inner), BF16),
        shape((rows, inner), BF16), shape((wrows, width), F32),
    )
    outputs = pl.pallas_call(
        functools.partial(whole_kernel, n, ndp, parts, 256, span),
        out_shape=out_shape[:4] + (shape((wrows, width), BF16),),
        in_specs=[pl.BlockSpec(memory_space=pltpu.SMEM)] + vmem(5),
        out_specs=tuple(vmem(5)),
        scratch_shapes=[
            pltpu.VMEM((slots, 5, seq, HD), BF16),
            pltpu.VMEM((slots, 4, seq, HD), BF16),
            pltpu.VMEM((slots, seq, seq), BF16),
            pltpu.VMEM((seq, seq), BF16),
            pltpu.VMEM((HD, seq), BF16),
            pltpu.VMEM((seq, HD), BF16),
            pltpu.VMEM((seq, HD), BF16),
            pltpu.VMEM((span * HD, width), BF16),
            pltpu.VMEM((ndp * rows, width), BF16),
            pltpu.VMEM((ndp * rows, span * HD), BF16),
            pltpu.VMEM((span * HD, ndp * rows), BF16),
            pltpu.VMEM((ndp, rows, span * HD), BF16),
            pltpu.VMEM((ndp * rows, width), BF16),
            pltpu.VMEM((ndp, rows, width), BF16),
            pltpu.VMEM((8, HD), F32),
            pltpu.VMEM((half, width), BF16),
            pltpu.VMEM((half, width), BF16),
            pltpu.VMEM((half, wide), F32),
            pltpu.VMEM((half, width), BF16),
            pltpu.VMEM((half, width), BF16),
            pltpu.VMEM((half, width), BF16),
            dma((3, HEADS)), dma((slots, 3)), dma((max(ndp, 6),)), dma((max(ndp, 6),)),
            dma((ndp, span)), dma((slots, 2)), dma((slots, n, 2)), dma((ndp, span)),
            dma((4, slots, n)), dma((4, HEADS)),
            dma((parts, ndp)), dma((parts, ndp)), dma((parts,)), dma((parts,)),
            dma((parts,)), dma((parts,)), dma((parts,)), dma((parts,)), dma((parts,)), dma((parts,)), dma((parts,)),
        ],
        compiler_params=pltpu.CompilerParams(
            collective_id=0, has_side_effects=True, vmem_limit_bytes=VMEM_BYTES
        ),
    )(seg_lengths, queries[0], keys[0], values[0], out_grad[0], w_out)
    anywhere = [pl.BlockSpec(memory_space=pl.ANY)] * 5
    attended, query_grad, key_grad, value_grad, weight_grad = pl.pallas_call(
        copy_kernel,
        out_shape=out_shape,
        in_specs=anywhere,
        out_specs=tuple(anywhere),
        scratch_shapes=[pltpu.VMEM(x.shape, BF16) for x in out_shape]
        + [pltpu.VMEM((wrows, width), F32), dma((5,)), dma((5,))],
        compiler_params=pltpu.CompilerParams(vmem_limit_bytes=VMEM_BYTES),
    )(*outputs)
    return (attended[None], query_grad[None], key_grad[None], value_grad[None], weight_grad)


def solution(mesh):
    in_specs = (
        P("dp", "ctx", None),
        P("dp", "ctx", None),
        P("dp", "ctx", None),
        P("dp", None),
        P("dp", "ctx", None),
        P("dp", None),
    )
    out_specs = (
        P("dp", "ctx", None),
        P("dp", "ctx", None),
        P("dp", "ctx", None),
        P("dp", "ctx", None),
        P("dp", None),
    )
    return jax.shard_map(local, mesh=mesh, in_specs=in_specs, out_specs=out_specs, check_vma=False)
```

time: 156 us -> 127 us (0.81)
  the two profiles are of different devices: /device:TPU:17 before, /device:TPU:1 now
where the time goes in v1:
time: 127 us
  Pallas kernels  126 us (99%)
    pallas_call x1, Pallas kernels, local(): pl.pallas_call(functools.partial(whole_kernel, n, ndp, parts, 256, span),...  122 us
    pallas_call x1, Pallas kernels, local(): pl.pallas_call(copy_kernel, out_shape=out_shape, in_specs=anywhere, out_s...  3.96 us

profile of v1, /device:TPU:1, one launch (start us, length us, event | category | flops | bytes accessed | tf_op | source)
XLA Modules:
  0.0 126.5 jit_solution(8929008409098489706)
XLA Ops:
  0.6 121.9 %shard_map.101 = (bf16[128,2560]{1,0:T(8,128)(2,1)}, bf16[128,1280]{1,0:T(8,128)(2,1)}, bf16[128,1280]{1,0:T(8,128)(2,1)}, bf16[128,1280]{1,0:T(8,128)(2,1)}, bf16[320,2560]{1,0:T(8,128)(2,1)}) custom-call(s32[1,8]{1,0:T(1,128)} %seg_ref.1, bf16[128,1280]{1,0:T(8,128)(2,1)} %bitcast.9, bf16[128,1280]{1,0:T(8,128)(2,1)} %bitcast.10, ...), custom_call_target="tpu_custom_call" | custom-call | tf_op jit(solution)/shard_map/pallas_call | solution.py:558
  122.6 4.0 %shard_map.102 = (bf16[128,2560]{1,0:T(8,128)(2,1)}, bf16[128,1280]{1,0:T(8,128)(2,1)}, bf16[128,1280]{1,0:T(8,128)(2,1)}, bf16[128,1280]{1,0:T(8,128)(2,1)}, f32[320,2560]{1,0:T(8,128)}) custom-call(bf16[128,2560]{1,0:T(8,128)(2,1)} %get-tuple-element.15.refs_0_, bf16[128,1280]{1,0:T(8,128)(2,1)} %get-tuple-element.16.refs_1_, ...), custom_call_target="tpu_custom_call" | custom-call | tf_op jit(solution)/shard_map/pallas_call | solution.py:596

commit v2 on v1

v2 whole, which is shorter than its diff:
```python
import functools
import math

import jax
import jax.numpy as jnp
from jax import lax
from jax.experimental import pallas as pl
from jax.experimental.pallas import tpu as pltpu
from jax.sharding import PartitionSpec as P

HEADS = 10
HD = 128
MASKED_SCORE = -1e30
MESH = pl.DeviceIdType.MESH
BF16 = jnp.bfloat16
F32 = jnp.float32
VMEM_BYTES = 56 * 1024 * 1024


def owner_of(head, n):
    slot, place = divmod(head, n)
    if slot and 2 * place + 2 < n:
        place = 2 * place + 2
    return place, slot


def head_in_slot(me, slot, n):
    if slot == 0:
        return me, me < HEADS
    head, valid = 0, False
    for h in range(slot * n, min(HEADS, (slot + 1) * n)):
        place = owner_of(h, n)[0]
        head = jnp.where(me == place, h, head)
        valid = jnp.logical_or(valid, me == place)
    return head, valid


def dot_nt(a, b):
    return lax.dot_general(a, b, (((1,), (1,)), ((), ())), preferred_element_type=F32)


def dot_tn(a, b):
    return lax.dot_general(a, b, (((0,), (0,)), ((), ())), preferred_element_type=F32)


def dot_nn(a, b):
    return jnp.dot(a, b, preferred_element_type=F32)


def remote(src, dst, send, recv, dp, ctx):
    return pltpu.make_async_remote_copy(
        src_ref=src, dst_ref=dst, send_sem=send, recv_sem=recv, device_id=(dp, ctx), device_id_type=MESH
    )


def greet(n, ndp):
    me, dp = lax.axis_index("ctx"), lax.axis_index("dp")
    barrier = pltpu.get_barrier_semaphore()
    for down in range(ndp):
        for step in range(n):
            if down or step:
                pl.semaphore_signal(
                    barrier, inc=1, device_id=(lax.rem(dp + down, ndp), lax.rem(me + step, n)), device_id_type=MESH
                )
    pl.semaphore_wait(barrier, n * ndp - 1)


def whole_kernel(
    n, ndp, parts, cuts, block, piece,
    seg_ref, q_ref, k_ref, v_ref, og_ref, w_hbm,
    attended_ref, qg_ref, kg_ref, vg_ref, wg_ref,
    heads_ref, grads_ref, attention_ref, result_ref, probs_ref, dscore_ref, turned, query_mask, key_mask,
    w_ref, og_all, att_t, att_all, grad_ref, psend_buf, precv_buf,
    xsend_buf, xrecv_buf, own_sum, chain_buf, outer_buf, middle_buf,
    load_sem, send_sem, recv_sem, osend, orecv, gsend, grecv, asend, arecv, hsend, hrecv,
    psend, precv, xsend, xrecv, csend, crecv, mrecv, bsend, brecv, fsend, frecv,
):
    me, dp = lax.axis_index("ctx"), lax.axis_index("dp")
    core = lax.rem(me, 2)
    chip = me // 2
    chips = n // 2
    sibling = me + 1 - 2 * core
    slots, _, seq, _ = heads_ref.shape
    rows = q_ref.shape[0]
    width = og_ref.shape[1]
    wrows = w_ref.shape[0]
    half = wrows // 2
    wide = width // parts
    broad = width // cuts
    pieces = wrows // piece
    scale = 1.0 / math.sqrt(HD)

    def record_rows(record):
        return pl.ds(pl.multiple_of(record * rows, rows), rows)

    my_rows = record_rows(me)
    loads = (
        pltpu.make_async_copy(w_hbm, w_ref, load_sem.at[0]),
        pltpu.make_async_copy(og_ref, og_all.at[record_rows(dp)], load_sem.at[1]),
    )
    for load in loads:
        load.start()
    greet(n, ndp)

    def head_columns(head):
        if isinstance(head, int):
            return pl.ds(head * HD, HD)
        return pl.ds(pl.multiple_of(head * HD, HD), HD)

    def place_of(head):
        slot = head // n
        place = head - slot * n
        if slots > 1:
            moved = 2 * place + 2
            place = jnp.where(jnp.logical_and(slot > 0, moved < n), moved, place)
        return place, slot

    def send_head(tensor, source, head, start):
        place, slot = owner_of(head, n)
        columns = head_columns(head)
        landing = heads_ref.at[slot, tensor, my_rows]
        copy = remote(
            source.at[:, columns], landing, send_sem.at[tensor, head], recv_sem.at[slot, tensor], dp, place,
        )

        @pl.when(me != place)
        def _():
            if start:
                copy.start()
            else:
                copy.wait_send()

        if start:
            @pl.when(me == place)
            def _():
                pltpu.make_async_copy(source.at[:, columns], landing, recv_sem.at[slot, tensor]).start()

    def await_head(slot, tensor):
        waited = heads_ref.at[slot, tensor]
        pltpu.make_async_copy(waited, waited, recv_sem.at[slot, tensor]).wait()

    def og_copy(source, at, count, record, slot, peer):
        landed = pl.ds(pl.multiple_of(record * rows + at, 16), count)
        return remote(source, og_all.at[landed], osend.at[slot], orecv.at[slot], peer, me)

    def send_slot(slot):
        for tensor, source in enumerate((q_ref, k_ref, v_ref)):
            for head in range(slot * n, min(HEADS, slot * n + n)):
                send_head(tensor, source, head, True)

    spread = []
    if ndp == 4:
        cut = rows // 2
        across = dp + 1 - 2 * lax.rem(dp, 2)
        along = lax.rem(dp + 2, 4)
        corner = 3 - dp
        peers = (across, along, corner)
        for order in range(2):
            for axis, peer in enumerate((across, along)):
                part = order if axis == 0 else 1 - order
                spread.append(
                    og_copy(og_ref.at[pl.ds(part * cut, cut)], part * cut, cut, dp, 2 * axis + part, peer)
                )
    else:
        peers = tuple(lax.rem(dp + ndp - step, ndp) for step in range(1, ndp))
        for step in range(1, ndp):
            spread.append(og_copy(og_ref, 0, rows, dp, step, lax.rem(dp + step, ndp)))
    for copy in spread:
        copy.start()
    send_slot(0)

    def piece_place(spot):
        feature = dp * wrows + spot * piece
        head = feature // HD
        place, slot = place_of(head)
        return place, slot, feature - head * HD

    def grad_copy(step, record, spot):
        place, slot, inside = piece_place(spot)
        return remote(
            grad_ref.at[step, pl.ds(spot * piece, piece)],
            grads_ref.at[slot, pl.ds(pl.multiple_of(inside, 16), piece), my_rows],
            gsend.at[step, spot], grecv.at[slot, inside // piece], record, place,
        )

    def make_grad(step, record):
        grad_ref[step] = dot_nt(w_ref[...], og_all[record_rows(record), :]).astype(BF16)
        for spot in range(pieces):
            if step:
                grad_copy(step, record, spot).start()
            else:
                place, slot, inside = piece_place(spot)

                @pl.when(place == me)
                def _():
                    held = pl.ds(pl.multiple_of(inside, 16), piece)
                    grads_ref[slot, held, my_rows] = grad_ref[0, pl.ds(spot * piece, piece), :]

                @pl.when(place != me)
                def _():
                    grad_copy(0, record, spot).start()

    for load in loads:
        load.wait()
    make_grad(0, dp)

    @pl.loop(0, seq // block)
    def _(index):
        at = pl.ds(pl.multiple_of(index * block, block), block)
        position = lax.broadcasted_iota(jnp.int32, (block, HD), 0) + index * block
        lane = lax.broadcasted_iota(jnp.int32, (block, HD), 1)
        count = seg_ref.shape[1]
        end = jnp.int32(0)
        segment = jnp.zeros((block, HD), jnp.int32)
        for i in range(count):
            end = end + seg_ref[0, i]
            segment = segment + jnp.where(position >= end, 1, 0)
        query_mask[at, :] = jnp.where(segment == lane, 1.0, 0.0).astype(BF16)
        key_mask[at, :] = jnp.where(jnp.logical_or(segment == lane, lane >= count), 0.0, MASKED_SCORE).astype(BF16)

    def await_og(slot, at, count, record):
        landed = og_all.at[pl.ds(pl.multiple_of(record * rows + at, 16), count)]
        remote(landed, landed, osend.at[0], orecv.at[slot], dp, me).wait_recv()
        return landed

    if ndp == 4:
        for axis, (peer, other) in enumerate(((across, along), (along, across))):
            landed = await_og(3 * axis, axis * cut, cut, peer)
            copy = og_copy(landed, axis * cut, cut, peer, 4 + axis, other)
            copy.start()
            spread.append(copy)
    for slot in range(1, slots):
        send_slot(slot)
    if ndp == 4:
        for axis, peer in enumerate((across, along)):
            await_og(axis + 1, (1 - axis) * cut, cut, peer)
            make_grad(axis + 1, peer)
    else:
        for step, peer in enumerate(peers, 1):
            await_og(step, 0, rows, peer)
            make_grad(step, peer)

    def attention_copy(slot, other, spot):
        head, _ = head_in_slot(me, slot, n)
        feature = head * HD + spot * piece
        target = feature // wrows
        row = feature - target * wrows
        landing = att_t.at[pl.ds(pl.multiple_of(row, 16), piece), record_rows(dp)]
        return target, landing, remote(
            attention_ref.at[slot, pl.ds(spot * piece, piece), record_rows(other)], landing,
            asend.at[slot, other, spot], arecv.at[dp, row // piece], target, other,
        )

    def attention_copies(slot, other, start):
        for spot in range(HD // piece):
            target, landing, copy = attention_copy(slot, other, spot)
            here = jnp.logical_and(target == dp, other == me)

            @pl.when(jnp.logical_not(here))
            def _():
                if start:
                    copy.start()
                else:
                    copy.wait_send()

            if start:
                @pl.when(here)
                def _():
                    landing[...] = attention_ref[slot, pl.ds(spot * piece, piece), my_rows]

    log2e = math.log2(math.e)

    def forward(slot):
        @pl.when(head_in_slot(me, slot, n)[1])
        def _():
            for tensor in range(3):
                await_head(slot, tensor)
            turned[...] = heads_ref[slot, 2].T

            @pl.loop(0, seq // block)
            def _(index):
                at = pl.ds(pl.multiple_of(index * block, block), block)
                left = jnp.concatenate([heads_ref[slot, 1], key_mask[...]], axis=1)
                right = jnp.concatenate([heads_ref[slot, 0, at, :], query_mask[at, :]], axis=1)
                scores = dot_nt(left, right)
                top = jnp.max(scores, axis=0, keepdims=True)
                shifted = jnp.exp2((scores - top) * (scale * log2e))
                total = jnp.sum(shifted, axis=0, keepdims=True)
                probs_b = (shifted * (1.0 / total)).astype(BF16)
                probs_ref[slot, :, at] = probs_b
                attention_ref[slot, :, at] = dot_nn(turned[...], probs_b).astype(BF16)
                for step in range(block // rows):
                    attention_copies(slot, index * (block // rows) + step, True)

    targets = (qg_ref, kg_ref, vg_ref)

    def home_copy(slot, tensor, other):
        head, _ = head_in_slot(me, slot, n)
        return remote(
            result_ref.at[slot, tensor, record_rows(other)], targets[tensor].at[:, head_columns(head)],
            hsend.at[tensor, slot, other], hrecv.at[tensor, head], dp, other,
        )

    def send_home(slot, tensor, other):
        @pl.when(other != me)
        def _():
            home_copy(slot, tensor, other).start()

        @pl.when(other == me)
        def _():
            head, _ = head_in_slot(me, slot, n)
            targets[tensor][:, head_columns(head)] = result_ref[slot, tensor, my_rows, :]

    def receive_home(tensor):
        for head in range(HEADS):
            place, _ = owner_of(head, n)

            @pl.when(me != place)
            def _():
                landed = targets[tensor].at[:, head_columns(head)]
                remote(landed, landed, hsend.at[tensor, 0, 0], hrecv.at[tensor, head], dp, place).wait_recv()

    def backward(slot):
        @pl.when(head_in_slot(me, slot, n)[1])
        def _():
            head, _ = head_in_slot(me, slot, n)
            turned[...] = heads_ref[slot, 1].T
            for spot in range(HD // piece):
                source = (head * HD + spot * piece) // wrows

                def await_grad(count):
                    waited = grads_ref.at[slot, pl.ds(spot * piece, piece), pl.ds(0, rows * count)]
                    pltpu.make_async_copy(waited, waited, grecv.at[slot, spot]).wait()

                pl.when(source == dp)(lambda: await_grad(n - 1))
                pl.when(source != dp)(lambda: await_grad(n))

            @pl.loop(0, seq // block)
            def _(index):
                at = pl.ds(pl.multiple_of(index * block, block), block)
                result_ref[slot, 2, at, :] = dot_nt(probs_ref[slot, at, :], grads_ref[slot]).astype(BF16)
                for step in range(block // rows):
                    send_home(slot, 2, index * (block // rows) + step)

            @pl.loop(0, seq // block)
            def _(index):
                at = pl.ds(pl.multiple_of(index * block, block), block)
                grad = grads_ref[slot, :, at]
                product = grad.astype(F32) * attention_ref[slot, :, at].astype(F32)
                grad_dot = jnp.sum(product, axis=0, keepdims=True)
                dprob = dot_nn(heads_ref[slot, 2], grad)
                dscore = (probs_ref[slot, :, at].astype(F32) * (dprob - grad_dot)).astype(BF16)
                dscore_ref[:, at] = dscore
                result_ref[slot, 0, at, :] = (dot_nn(turned[...], dscore) * scale).astype(BF16).T
                for step in range(block // rows):
                    send_home(slot, 0, index * (block // rows) + step)

            @pl.loop(0, seq // block)
            def _(index):
                at = pl.ds(pl.multiple_of(index * block, block), block)
                result_ref[slot, 1, at, :] = (dot_nn(dscore_ref[at, :], heads_ref[slot, 0]) * scale).astype(BF16)
                for step in range(block // rows):
                    send_home(slot, 1, index * (block // rows) + step)

    forward(0)
    if ndp == 4:
        for axis in range(2):
            await_og(4 + axis, axis * cut, cut, corner)
        make_grad(3, corner)
    for slot in range(1, slots):
        forward(slot)
    backward(0)

    for record in range(ndp):
        for spot in range(pieces):
            landed = att_t.at[pl.ds(spot * piece, piece), pl.ds(record * rows, rows)]
            here = jnp.logical_and(record == dp, piece_place(spot)[0] == me)

            @pl.when(jnp.logical_not(here))
            def _():
                remote(landed, landed, asend.at[0, 0, 0], arecv.at[record, spot], dp, sibling).wait_recv()

    def part_columns(part):
        return pl.ds(part * wide, wide)

    def cut_columns(part):
        return pl.ds(part * broad, broad)

    my_half = pl.ds(pl.multiple_of(core * half, 16), half)
    their_half = pl.ds(pl.multiple_of((1 - core) * half, 16), half)

    def pair_copy(part):
        columns = cut_columns(part)
        return remote(
            xsend_buf.at[:, columns], xrecv_buf.at[:, columns], xsend.at[part], xrecv.at[part], dp, sibling,
        )

    def partial_copy(part, step):
        columns = cut_columns(part)
        other = lax.rem(dp + step, ndp)
        return remote(
            psend_buf.at[record_rows(other), columns], precv_buf.at[step - 1, :, columns],
            psend.at[part, step], precv.at[part, step], other, me,
        )

    for part in range(cuts):
        columns = cut_columns(part)
        xsend_buf[:, columns] = dot_nn(att_t[their_half, :], og_all[:, columns]).astype(BF16)
        pair_copy(part).start()
    att_all[...] = att_t[...].T
    for part in range(cuts):
        columns = cut_columns(part)
        psend_buf[:, columns] = dot_nn(att_all[...], w_ref[:, columns]).astype(BF16)
        for step in range(1, ndp):
            partial_copy(part, step).start()
    for slot in range(1, slots):
        backward(slot)

    depth = jnp.where(chip < chips // 2, chip, chips - 1 - chip)
    toward = jnp.where(chip < chips // 2, 1, -1)
    innermost = depth == chips // 2 - 1
    inner = me + 2 * toward
    outer = me - 2 * toward

    def inward_copy(part):
        columns = part_columns(part)
        return remote(
            chain_buf.at[:, columns], outer_buf.at[:, columns], csend.at[part], crecv.at[part], dp, inner,
        )

    def middle_copy(part):
        columns = part_columns(part)
        return remote(
            chain_buf.at[:, columns], middle_buf.at[:, columns], csend.at[part], mrecv.at[part], dp, inner,
        )

    def outward_copy(part):
        landed = wg_ref.at[my_half, part_columns(part)]
        return remote(landed, landed, bsend.at[part], brecv.at[part], dp, outer)

    def pass_copy(part, held):
        landed = wg_ref.at[held, part_columns(part)]
        return remote(landed, landed, fsend.at[part], frecv.at[part], dp, sibling)

    def hand_on(part):
        @pl.when(depth > 0)
        def _():
            outward_copy(part).start()

        pass_copy(part, my_half).start()

    def finish_inner(part):
        @pl.when(innermost)
        def _():
            columns = part_columns(part)
            middle_copy(part).wait_recv()
            total = chain_buf[:, columns].astype(F32) + middle_buf[:, columns].astype(F32)
            wg_ref[my_half, columns] = total.astype(BF16)
            hand_on(part)

    lag = 2
    for part in range(parts):
        columns = part_columns(part)
        own_sum[...] = dot_nn(att_t[my_half, :], og_all[:, columns])
        if part * wide % broad == 0:
            pair_copy(part * wide // broad).wait_recv()
        own_sum[...] += xrecv_buf[:, columns].astype(F32)

        @pl.when(depth > 0)
        def _():
            inward_copy(part).wait_recv()
            own_sum[...] += outer_buf[:, columns].astype(F32)

        chain_buf[:, columns] = own_sum[...].astype(BF16)
        if part >= lag:
            inward_copy(part - lag).wait_send()

        @pl.when(innermost)
        def _():
            middle_copy(part).start()

        @pl.when(jnp.logical_not(innermost))
        def _():
            inward_copy(part).start()

        if part >= lag:
            finish_inner(part - lag)
    for part in range(parts - lag, parts):
        finish_inner(part)

    for part in range(cuts):
        columns = cut_columns(part)
        total = psend_buf[record_rows(dp), columns].astype(F32)
        for step in range(1, ndp):
            partial_copy(part, step).wait_recv()
            total = total + precv_buf[step - 1, :, columns].astype(F32)
        attended_ref[:, columns] = total.astype(BF16)

    for part in range(parts):
        @pl.when(jnp.logical_not(innermost))
        def _():
            outward_copy(part).wait_recv()
            hand_on(part)

    for tensor in range(3):
        receive_home(tensor)
    for part in range(parts):
        pass_copy(part, their_half).wait_recv()

    for tensor, source in enumerate((q_ref, k_ref, v_ref)):
        for head in range(HEADS):
            send_head(tensor, source, head, False)
    for copy in spread:
        copy.wait_send()
    for step, record in enumerate((dp,) + peers):
        for spot in range(pieces):
            copy = grad_copy(step, record, spot)
            if step:
                copy.wait_send()
            else:
                pl.when(piece_place(spot)[0] != me)(copy.wait_send)
    for slot in range(slots):
        @pl.when(head_in_slot(me, slot, n)[1])
        def _():
            for other in range(n):
                attention_copies(slot, other, False)
                for tensor in range(3):
                    pl.when(other != me)(home_copy(slot, tensor, other).wait_send)
    for part in range(cuts):
        pair_copy(part).wait_send()
        for step in range(1, ndp):
            partial_copy(part, step).wait_send()
    for part in range(parts):
        if part >= parts - lag:
            inward_copy(part).wait_send()
        pl.when(depth > 0)(outward_copy(part).wait_send)
        pass_copy(part, my_half).wait_send()


def copy_kernel(*refs):
    sources, targets, held = refs[:5], refs[5:10], refs[10:15]
    wide_held, in_sem, out_sem = refs[15:]
    loads = [pltpu.make_async_copy(sources[i], held[i], in_sem.at[i]) for i in range(5)]
    stores = [
        pltpu.make_async_copy(held[i] if i < 4 else wide_held, targets[i], out_sem.at[i]) for i in range(5)
    ]
    for i in (4, 0, 1, 2, 3):
        loads[i].start()
    loads[4].wait()
    wide_held[...] = held[4][...].astype(F32)
    stores[4].start()
    for i in range(4):
        loads[i].wait()
        stores[i].start()
    for store in stores:
        store.wait()


def vmem(count):
    return [pl.BlockSpec(memory_space=pltpu.VMEM)] * count


def local(queries, keys, values, seg_lengths, out_grad, w_out):
    n, ndp = lax.axis_size("ctx"), lax.axis_size("dp")
    rows, inner = queries.shape[1:]
    width = out_grad.shape[2]
    seq = rows * n
    wrows = w_out.shape[0]
    half = wrows // 2
    slots = -(-HEADS // n)
    parts, cuts = 10, 5
    wide = width // parts
    piece = math.gcd(HD, wrows)
    shape = jax.ShapeDtypeStruct
    dma = pltpu.SemaphoreType.DMA
    out_shape = (
        shape((rows, width), BF16), shape((rows, inner), BF16), shape((rows, inner), BF16),
        shape((rows, inner), BF16), shape((wrows, width), F32),
    )
    anywhere = [pl.BlockSpec(memory_space=pl.ANY)] * 5
    outputs = pl.pallas_call(
        functools.partial(whole_kernel, n, ndp, parts, cuts, 256, piece),
        out_shape=out_shape[:4] + (shape((wrows, width), BF16),),
        in_specs=[pl.BlockSpec(memory_space=pltpu.SMEM)] + anywhere,
        out_specs=tuple(vmem(5)),
        scratch_shapes=[
            pltpu.VMEM((slots, 3, seq, HD), BF16),
            pltpu.VMEM((slots, HD, seq), BF16),
            pltpu.VMEM((slots, HD, seq), BF16),
            pltpu.VMEM((slots, 3, seq, HD), BF16),
            pltpu.VMEM((slots, seq, seq), BF16),
            pltpu.VMEM((seq, seq), BF16),
            pltpu.VMEM((HD, seq), BF16),
            pltpu.VMEM((seq, HD), BF16),
            pltpu.VMEM((seq, HD), BF16),
            pltpu.VMEM((wrows, width), BF16),
            pltpu.VMEM((ndp * rows, width), BF16),
            pltpu.VMEM((wrows, ndp * rows), BF16),
            pltpu.VMEM((ndp * rows, wrows), BF16),
            pltpu.VMEM((ndp, wrows, rows), BF16),
            pltpu.VMEM((ndp * rows, width), BF16),
            pltpu.VMEM((ndp - 1, rows, width), BF16),
            pltpu.VMEM((half, width), BF16),
            pltpu.VMEM((half, width), BF16),
            pltpu.VMEM((half, wide), F32),
            pltpu.VMEM((half, width), BF16),
            pltpu.VMEM((half, width), BF16),
            pltpu.VMEM((half, width), BF16),
            dma((2,)), dma((3, HEADS)), dma((slots, 3)), dma((max(ndp, 6),)), dma((max(ndp, 6),)),
            dma((ndp, wrows // piece)), dma((slots, HD // piece)), dma((slots, n, HD // piece)), dma((ndp, wrows // piece)),
            dma((3, slots, n)), dma((3, HEADS)),
            dma((cuts, ndp)), dma((cuts, ndp)), dma((cuts,)), dma((cuts,)),
            dma((parts,)), dma((parts,)), dma((parts,)), dma((parts,)), dma((parts,)), dma((parts,)), dma((parts,)),
        ],
        compiler_params=pltpu.CompilerParams(
            collective_id=0, has_side_effects=True, vmem_limit_bytes=VMEM_BYTES
        ),
    )(seg_lengths, queries[0], keys[0], values[0], out_grad[0], w_out)
    attended, query_grad, key_grad, value_grad, weight_grad = pl.pallas_call(
        copy_kernel,
        out_shape=out_shape,
        in_specs=anywhere,
        out_specs=tuple(anywhere),
        scratch_shapes=[pltpu.VMEM(x.shape, BF16) for x in out_shape]
        + [pltpu.VMEM((wrows, width), F32), dma((5,)), dma((5,))],
        compiler_params=pltpu.CompilerParams(vmem_limit_bytes=VMEM_BYTES),
    )(*outputs)
    return (attended[None], query_grad[None], key_grad[None], value_grad[None], weight_grad)


def solution(mesh):
    in_specs = (
        P("dp", "ctx", None),
        P("dp", "ctx", None),
        P("dp", "ctx", None),
        P("dp", None),
        P("dp", "ctx", None),
        P("dp", None),
    )
    out_specs = (
        P("dp", "ctx", None),
        P("dp", "ctx", None),
        P("dp", "ctx", None),
        P("dp", "ctx", None),
        P("dp", None),
    )
    return jax.shard_map(local, mesh=mesh, in_specs=in_specs, out_specs=out_specs, check_vma=False)
```

time: 127 us -> 106 us (0.83)
  Pallas kernels: 126 us -> 105 us
    pallas_call x1, Pallas kernels: 122 us -> 101 us  [local(): pl.pallas_call(functools.partial(whole_kernel, n, ndp, parts, cuts, 256,...]
where the time goes in v2:
time: 106 us
  Pallas kernels  105 us (99%)
    pallas_call x1, Pallas kernels, local(): pl.pallas_call(functools.partial(whole_kernel, n, ndp, parts, cuts, 256,...  101 us
    pallas_call x1, Pallas kernels, local(): pl.pallas_call(copy_kernel, out_shape=out_shape, in_specs=anywhere, out_s...  3.96 us

profile of v2, /device:TPU:1, one launch (start us, length us, event | category | flops | bytes accessed | tf_op | source)
XLA Modules:
  0.0 106.0 jit_solution(15811845547415083973)
XLA Ops:
  0.6 101.4 %shard_map.101 = (bf16[128,2560]{1,0:T(8,128)(2,1)}, bf16[128,1280]{1,0:T(8,128)(2,1)}, bf16[128,1280]{1,0:T(8,128)(2,1)}, bf16[128,1280]{1,0:T(8,128)(2,1)}, bf16[320,2560]{1,0:T(8,128)(2,1)}) custom-call(s32[1,8]{1,0:T(1,128)} %seg_ref.1, bf16[128,1280]{1,0:T(8,128)(2,1)} %bitcast.9, bf16[128,1280]{1,0:T(8,128)(2,1)} %bitcast.10, ...), custom_call_target="tpu_custom_call" | custom-call | tf_op jit(solution)/shard_map/pallas_call | solution.py:581
  102.0 4.0 %shard_map.102 = (bf16[128,2560]{1,0:T(8,128)(2,1)}, bf16[128,1280]{1,0:T(8,128)(2,1)}, bf16[128,1280]{1,0:T(8,128)(2,1)}, bf16[128,1280]{1,0:T(8,128)(2,1)}, f32[320,2560]{1,0:T(8,128)}) custom-call(bf16[128,2560]{1,0:T(8,128)(2,1)} %get-tuple-element.15.refs_0_, bf16[128,1280]{1,0:T(8,128)(2,1)} %get-tuple-element.16.refs_1_, ...), custom_call_target="tpu_custom_call" | custom-call | tf_op jit(solution)/shard_map/pallas_call | solution.py:619

commit v3 on v2

--- a/solution.py
+++ b/solution.py
@@ -68,12 +68,12 @@
 def whole_kernel(
     n, ndp, parts, cuts, block, piece,
     seg_ref, q_ref, k_ref, v_ref, og_ref, w_hbm,
-    attended_ref, qg_ref, kg_ref, vg_ref, wg_ref,
+    attended_out, qg_ref, kg_ref, vg_ref, wg_out,
     heads_ref, grads_ref, attention_ref, result_ref, probs_ref, dscore_ref, turned, query_mask, key_mask,
     w_ref, og_all, att_t, att_all, grad_ref, psend_buf, precv_buf,
-    xsend_buf, xrecv_buf, own_sum, chain_buf, outer_buf, middle_buf,
+    xsend_buf, xrecv_buf, own_sum, chain_buf, outer_buf, middle_buf, wg_ref, att_sum,
     load_sem, send_sem, recv_sem, osend, orecv, gsend, grecv, asend, arecv, hsend, hrecv,
-    psend, precv, xsend, xrecv, csend, crecv, mrecv, bsend, brecv, fsend, frecv,
+    psend, precv, xsend, xrecv, csend, crecv, mrecv, bsend, brecv, fsend, frecv, store_sem, wide_sem,
 ):
     me, dp = lax.axis_index("ctx"), lax.axis_index("dp")
     core = lax.rem(me, 2)
@@ -185,6 +185,8 @@
 
     def make_grad(step, record):
         grad_ref[step] = dot_nt(w_ref[...], og_all[record_rows(record), :]).astype(BF16)
+
+    def send_grad(step, record):
         for spot in range(pieces):
             if step:
                 grad_copy(step, record, spot).start()
@@ -309,16 +311,13 @@
         @pl.when(other == me)
         def _():
             head, _ = head_in_slot(me, slot, n)
-            targets[tensor][:, head_columns(head)] = result_ref[slot, tensor, my_rows, :]
+            landing = targets[tensor].at[:, head_columns(head)]
+            pltpu.make_async_copy(result_ref.at[slot, tensor, my_rows], landing, hrecv.at[tensor, head]).start()
 
     def receive_home(tensor):
         for head in range(HEADS):
-            place, _ = owner_of(head, n)
-
-            @pl.when(me != place)
-            def _():
-                landed = targets[tensor].at[:, head_columns(head)]
-                remote(landed, landed, hsend.at[tensor, 0, 0], hrecv.at[tensor, head], dp, place).wait_recv()
+            landed = targets[tensor].at[:, head_columns(head)]
+            pltpu.make_async_copy(landed, landed, hrecv.at[tensor, head]).wait()
 
     def backward(slot):
         @pl.when(head_in_slot(me, slot, n)[1])
@@ -352,24 +351,28 @@
                 dscore = (probs_ref[slot, :, at].astype(F32) * (dprob - grad_dot)).astype(BF16)
                 dscore_ref[:, at] = dscore
                 result_ref[slot, 0, at, :] = (dot_nn(turned[...], dscore) * scale).astype(BF16).T
-                for step in range(block // rows):
-                    send_home(slot, 0, index * (block // rows) + step)
 
             @pl.loop(0, seq // block)
             def _(index):
                 at = pl.ds(pl.multiple_of(index * block, block), block)
                 result_ref[slot, 1, at, :] = (dot_nn(dscore_ref[at, :], heads_ref[slot, 0]) * scale).astype(BF16)
-                for step in range(block // rows):
-                    send_home(slot, 1, index * (block // rows) + step)
-
-    forward(0)
+
+    def send_some(slot, tensor, others):
+        @pl.when(head_in_slot(me, slot, n)[1])
+        def _():
+            for other in others:
+                send_home(slot, tensor, other)
+
+    for slot in range(slots):
+        forward(slot)
+    for step, record in enumerate((dp,) + peers[:2]):
+        send_grad(step, record)
     if ndp == 4:
         for axis in range(2):
             await_og(4 + axis, axis * cut, cut, corner)
         make_grad(3, corner)
-    for slot in range(1, slots):
-        forward(slot)
-    backward(0)
+    for step, record in enumerate(peers[2:], 3):
+        send_grad(step, record)
 
     for record in range(ndp):
         for spot in range(pieces):
@@ -395,27 +398,45 @@
             xsend_buf.at[:, columns], xrecv_buf.at[:, columns], xsend.at[part], xrecv.at[part], dp, sibling,
         )
 
-    def partial_copy(part, step):
+    def partial_copy(part, step, source, other):
         columns = cut_columns(part)
-        other = lax.rem(dp + step, ndp)
         return remote(
-            psend_buf.at[record_rows(other), columns], precv_buf.at[step - 1, :, columns],
+            psend_buf.at[record_rows(source), columns], precv_buf.at[step - 1, :, columns],
             psend.at[part, step], precv.at[part, step], other, me,
         )
 
+    def partial_copies(part):
+        if ndp == 4:
+            near, far = (across, along) if 2 * part < cuts else (along, across)
+            moves = ((near, near), (corner, near), (far, far))
+        else:
+            moves = tuple((lax.rem(dp + step, ndp),) * 2 for step in range(1, ndp))
+        return tuple(functools.partial(partial_copy, part, step, *move) for step, move in enumerate(moves, 1))
+
+    def partial_relay(part):
+        far = along if 2 * part < cuts else across
+        columns = cut_columns(part)
+        copies = partial_copies(part)
+        copies[1]().wait_recv()
+        held = record_rows(far)
+        total = psend_buf[held, columns].astype(F32) + precv_buf[1, :, columns].astype(F32)
+        psend_buf[held, columns] = total.astype(BF16)
+        copies[2]().start()
+
     for part in range(cuts):
         columns = cut_columns(part)
-        xsend_buf[:, columns] = dot_nn(att_t[their_half, :], og_all[:, columns]).astype(BF16)
+        product = dot_nn(att_t[...], og_all[:, columns])
+        low, high = product[:half], product[half:]
+        xsend_buf[:, columns] = jnp.where(core == 0, high, low).astype(BF16)
+        own_sum[:, columns] = jnp.where(core == 0, low, high)
         pair_copy(part).start()
     att_all[...] = att_t[...].T
-    for part in range(cuts):
+    order = [part for pair in zip(range(cuts // 2), range(cuts // 2, cuts)) for part in pair]
+    for part in order:
         columns = cut_columns(part)
         psend_buf[:, columns] = dot_nn(att_all[...], w_ref[:, columns]).astype(BF16)
-        for step in range(1, ndp):
-            partial_copy(part, step).start()
-    for slot in range(1, slots):
-        backward(slot)
-
+        for copy in partial_copies(part)[: 2 if ndp == 4 else ndp]:
+            copy().start()
     depth = jnp.where(chip < chips // 2, chip, chips - 1 - chip)
     toward = jnp.where(chip < chips // 2, 1, -1)
     innermost = depth == chips // 2 - 1
@@ -435,12 +456,20 @@
         )
 
     def outward_copy(part):
-        landed = wg_ref.at[my_half, part_columns(part)]
+        landed = wg_ref.at[:, part_columns(part)]
         return remote(landed, landed, bsend.at[part], brecv.at[part], dp, outer)
 
     def pass_copy(part, held):
-        landed = wg_ref.at[held, part_columns(part)]
-        return remote(landed, landed, fsend.at[part], frecv.at[part], dp, sibling)
+        columns = part_columns(part)
+        return remote(wg_ref.at[:, columns], wg_out.at[held, columns], fsend.at[part], frecv.at[part], dp, sibling)
+
+    def wide_store(part):
+        columns = part_columns(part)
+        return pltpu.make_async_copy(wg_ref.at[:, columns], wg_out.at[my_half, columns], wide_sem.at[part])
+
+    def store(part):
+        columns = cut_columns(part)
+        return pltpu.make_async_copy(att_sum.at[:, columns], attended_out.at[:, columns], store_sem.at[part])
 
     def hand_on(part):
         @pl.when(depth > 0)
@@ -448,53 +477,74 @@
             outward_copy(part).start()
 
         pass_copy(part, my_half).start()
+        wide_store(part).start()
 
     def finish_inner(part):
-        @pl.when(innermost)
-        def _():
-            columns = part_columns(part)
-            middle_copy(part).wait_recv()
-            total = chain_buf[:, columns].astype(F32) + middle_buf[:, columns].astype(F32)
-            wg_ref[my_half, columns] = total.astype(BF16)
-            hand_on(part)
+        columns = part_columns(part)
+        middle_copy(part).wait_recv()
+        total = chain_buf[:, columns].astype(F32) + middle_buf[:, columns].astype(F32)
+        wg_ref[:, columns] = total.astype(BF16)
+        hand_on(part)
+
+    def chain_sum(part):
+        columns = part_columns(part)
+        for waited in range(cuts):
+            if part * wide <= waited * broad < (part + 1) * wide:
+                pair_copy(waited).wait_recv()
+        own_sum[:, columns] += xrecv_buf[:, columns].astype(F32)
+
+        @pl.when(depth > 0)
+        def _():
+            inward_copy(part).wait_recv()
+            own_sum[:, columns] += outer_buf[:, columns].astype(F32)
+
+        chain_buf[:, columns] = own_sum[:, columns].astype(BF16)
+
+    @pl.when(jnp.logical_not(innermost))
+    def _():
+        for part in range(parts):
+            chain_sum(part)
+            inward_copy(part).start()
+
+    for slot in range(slots):
+        backward(slot)
+        send_some(slot, 0, range(n))
 
     lag = 2
-    for part in range(parts):
-        columns = part_columns(part)
-        own_sum[...] = dot_nn(att_t[my_half, :], og_all[:, columns])
-        if part * wide % broad == 0:
-            pair_copy(part * wide // broad).wait_recv()
-        own_sum[...] += xrecv_buf[:, columns].astype(F32)
-
-        @pl.when(depth > 0)
-        def _():
-            inward_copy(part).wait_recv()
-            own_sum[...] += outer_buf[:, columns].astype(F32)
-
-        chain_buf[:, columns] = own_sum[...].astype(BF16)
-        if part >= lag:
-            inward_copy(part - lag).wait_send()
-
-        @pl.when(innermost)
-        def _():
+
+    @pl.when(innermost)
+    def _():
+        for part in range(parts):
+            chain_sum(part)
+            if part >= lag:
+                middle_copy(part - lag).wait_send()
             middle_copy(part).start()
-
-        @pl.when(jnp.logical_not(innermost))
-        def _():
-            inward_copy(part).start()
-
-        if part >= lag:
-            finish_inner(part - lag)
-    for part in range(parts - lag, parts):
-        finish_inner(part)
-
-    for part in range(cuts):
+            if part >= lag:
+                finish_inner(part - lag)
+            for slot in range(slots):
+                send_some(slot, 1, range(part * n // parts, (part + 1) * n // parts))
+            if ndp == 4 and part >= parts - cuts:
+                partial_relay(order[part - parts + cuts])
+        for part in range(parts - lag, parts):
+            finish_inner(part)
+
+    @pl.when(jnp.logical_not(innermost))
+    def _():
+        for slot in range(slots):
+            send_some(slot, 1, range(n))
+        if ndp == 4:
+            for part in order:
+                partial_relay(part)
+
+    for part in order:
         columns = cut_columns(part)
         total = psend_buf[record_rows(dp), columns].astype(F32)
-        for step in range(1, ndp):
-            partial_copy(part, step).wait_recv()
-            total = total + precv_buf[step - 1, :, columns].astype(F32)
-        attended_ref[:, columns] = total.astype(BF16)
+        for step, copy in enumerate(partial_copies(part)):
+            if ndp != 4 or step != 1:
+                copy().wait_recv()
+                total = total + precv_buf[step, :, columns].astype(F32)
+        att_sum[:, columns] = total.astype(BF16)
+        store(part).start()
 
     for part in range(parts):
         @pl.when(jnp.logical_not(innermost))
@@ -528,36 +578,41 @@
                     pl.when(other != me)(home_copy(slot, tensor, other).wait_send)
     for part in range(cuts):
         pair_copy(part).wait_send()
-        for step in range(1, ndp):
-            partial_copy(part, step).wait_send()
+        for copy in partial_copies(part):
+            copy().wait_send()
     for part in range(parts):
         if part >= parts - lag:
             inward_copy(part).wait_send()
+        else:
+            pl.when(jnp.logical_not(innermost))(inward_copy(part).wait_send)
         pl.when(depth > 0)(outward_copy(part).wait_send)
         pass_copy(part, my_half).wait_send()
-
-
-def copy_kernel(*refs):
+        wide_store(part).wait()
+    for part in range(cuts):
+        store(part).wait()
+
+
+def copy_kernel(pieces, *refs):
     sources, targets, held = refs[:5], refs[5:10], refs[10:15]
     wide_held, in_sem, out_sem = refs[15:]
-    loads = [pltpu.make_async_copy(sources[i], held[i], in_sem.at[i]) for i in range(5)]
+    spans = []
+    for i in (4, 0, 1, 2, 3):
+        rows = held[i].shape[0] // (pieces if i == 4 else 2)
+        spans += [(i, pl.ds(at, rows)) for at in range(0, held[i].shape[0], rows)]
+    loads = [pltpu.make_async_copy(sources[i].at[x], held[i].at[x], in_sem.at[j]) for j, (i, x) in enumerate(spans)]
     stores = [
-        pltpu.make_async_copy(held[i] if i < 4 else wide_held, targets[i], out_sem.at[i]) for i in range(5)
+        pltpu.make_async_copy((held[i] if i < 4 else wide_held).at[x], targets[i].at[x], out_sem.at[j])
+        for j, (i, x) in enumerate(spans)
     ]
-    for i in (4, 0, 1, 2, 3):
-        loads[i].start()
-    loads[4].wait()
-    wide_held[...] = held[4][...].astype(F32)
-    stores[4].start()
-    for i in range(4):
-        loads[i].wait()
-        stores[i].start()
+    for load in loads:
+        load.start()
+    for j, (i, x) in enumerate(spans):
+        loads[j].wait()
+        if i == 4:
+            wide_held[x, :] = held[4][x, :].astype(F32)
+        stores[j].start()
     for store in stores:
         store.wait()
-
-
-def vmem(count):
-    return [pl.BlockSpec(memory_space=pltpu.VMEM)] * count
 
 
 def local(queries, keys, values, seg_lengths, out_grad, w_out):
@@ -568,8 +623,8 @@
     wrows = w_out.shape[0]
     half = wrows // 2
     slots = -(-HEADS // n)
-    parts, cuts = 10, 5
-    wide = width // parts
+    parts, cuts = 10, 4
+    block = math.gcd(512, seq)
     piece = math.gcd(HD, wrows)
     shape = jax.ShapeDtypeStruct
     dma = pltpu.SemaphoreType.DMA
@@ -579,10 +634,10 @@
     )
     anywhere = [pl.BlockSpec(memory_space=pl.ANY)] * 5
     outputs = pl.pallas_call(
-        functools.partial(whole_kernel, n, ndp, parts, cuts, 256, piece),
+        functools.partial(whole_kernel, n, ndp, parts, cuts, block, piece),
         out_shape=out_shape[:4] + (shape((wrows, width), BF16),),
         in_specs=[pl.BlockSpec(memory_space=pltpu.SMEM)] + anywhere,
-        out_specs=tuple(vmem(5)),
+        out_specs=tuple(anywhere),
         scratch_shapes=[
             pltpu.VMEM((slots, 3, seq, HD), BF16),
             pltpu.VMEM((slots, HD, seq), BF16),
@@ -602,27 +657,30 @@
             pltpu.VMEM((ndp - 1, rows, width), BF16),
             pltpu.VMEM((half, width), BF16),
             pltpu.VMEM((half, width), BF16),
-            pltpu.VMEM((half, wide), F32),
+            pltpu.VMEM((half, width), F32),
             pltpu.VMEM((half, width), BF16),
             pltpu.VMEM((half, width), BF16),
             pltpu.VMEM((half, width), BF16),
+            pltpu.VMEM((half, width), BF16),
+            pltpu.VMEM((rows, width), BF16),
             dma((2,)), dma((3, HEADS)), dma((slots, 3)), dma((max(ndp, 6),)), dma((max(ndp, 6),)),
             dma((ndp, wrows // piece)), dma((slots, HD // piece)), dma((slots, n, HD // piece)), dma((ndp, wrows // piece)),
             dma((3, slots, n)), dma((3, HEADS)),
             dma((cuts, ndp)), dma((cuts, ndp)), dma((cuts,)), dma((cuts,)),
             dma((parts,)), dma((parts,)), dma((parts,)), dma((parts,)), dma((parts,)), dma((parts,)), dma((parts,)),
+            dma((cuts,)), dma((parts,)),
         ],
         compiler_params=pltpu.CompilerParams(
             collective_id=0, has_side_effects=True, vmem_limit_bytes=VMEM_BYTES
         ),
     )(seg_lengths, queries[0], keys[0], values[0], out_grad[0], w_out)
     attended, query_grad, key_grad, value_grad, weight_grad = pl.pallas_call(
-        copy_kernel,
+        functools.partial(copy_kernel, 5),
         out_shape=out_shape,
         in_specs=anywhere,
         out_specs=tuple(anywhere),
         scratch_shapes=[pltpu.VMEM(x.shape, BF16) for x in out_shape]
-        + [pltpu.VMEM((wrows, width), F32), dma((5,)), dma((5,))],
+        + [pltpu.VMEM((wrows, width), F32), dma((13,)), dma((13,))],
         compiler_params=pltpu.CompilerParams(vmem_limit_bytes=VMEM_BYTES),
     )(*outputs)
     return (attended[None], query_grad[None], key_grad[None], value_grad[None], weight_grad)

time: 106 us -> 103 us (0.972)
  Pallas kernels: 105 us -> 102 us
    pallas_call x2, Pallas kernels: 105 us -> 102 us  [the longest x1 98.6 us: local(): pl.pallas_call(functools.partial(whole_kernel, n, ndp, parts, cuts, block...]
where the time goes in v3:
time: 103 us
  Pallas kernels  102 us (99%)
    pallas_call x1, Pallas kernels, local(): pl.pallas_call(functools.partial(whole_kernel, n, ndp, parts, cuts, block...  98.6 us
    pallas_call x1, Pallas kernels, local(): pl.pallas_call(functools.partial(copy_kernel, 5), out_shape=out_shape, in...  3.46 us

profile of v3, /device:TPU:1, one launch (start us, length us, event | category | flops | bytes accessed | tf_op | source)
XLA Modules:
  0.0 102.7 jit_solution(10488518940206179790)
XLA Ops:
  0.6 98.6 %shard_map.101 = (bf16[128,2560]{1,0:T(8,128)(2,1)}, bf16[128,1280]{1,0:T(8,128)(2,1)}, bf16[128,1280]{1,0:T(8,128)(2,1)}, bf16[128,1280]{1,0:T(8,128)(2,1)}, bf16[320,2560]{1,0:T(8,128)(2,1)}) custom-call(s32[1,8]{1,0:T(1,128)} %seg_ref.1, bf16[128,1280]{1,0:T(8,128)(2,1)} %bitcast.9, bf16[128,1280]{1,0:T(8,128)(2,1)} %bitcast.10, ...), custom_call_target="tpu_custom_call" | custom-call | tf_op jit(solution)/shard_map/pallas_call | solution.py:636
  99.2 3.5 %shard_map.102 = (bf16[128,2560]{1,0:T(8,128)(2,1)}, bf16[128,1280]{1,0:T(8,128)(2,1)}, bf16[128,1280]{1,0:T(8,128)(2,1)}, bf16[128,1280]{1,0:T(8,128)(2,1)}, f32[320,2560]{1,0:T(8,128)}) custom-call(bf16[128,2560]{1,0:T(8,128)(2,1)} %get-tuple-element.15.refs_0_, bf16[128,1280]{1,0:T(8,128)(2,1)} %get-tuple-element.16.refs_1_, ...), custom_call_target="tpu_custom_call" | custom-call | tf_op jit(solution)/shard_map/pallas_call | solution.py:677

commit v4 on v3

--- a/solution.py
+++ b/solution.py
@@ -510,7 +510,7 @@
         backward(slot)
         send_some(slot, 0, range(n))
 
-    lag = 2
+    lag = 4
 
     @pl.when(innermost)
     def _():

time: 103 us -> 103 us (level)
  no operation moved by 1% of the time
where the time goes in v4:
time: 103 us
  Pallas kernels  102 us (99%)
    pallas_call x1, Pallas kernels, local(): pl.pallas_call(functools.partial(whole_kernel, n, ndp, parts, cuts, block...  98.6 us
    pallas_call x1, Pallas kernels, local(): pl.pallas_call(functools.partial(copy_kernel, 5), out_shape=out_shape, in...  3.46 us

profile of v4, /device:TPU:1, one launch (start us, length us, event | category | flops | bytes accessed | tf_op | source)
XLA Modules:
  0.0 102.7 jit_solution(12444246059968374451)
XLA Ops:
  0.6 98.6 %shard_map.101 = (bf16[128,2560]{1,0:T(8,128)(2,1)}, bf16[128,1280]{1,0:T(8,128)(2,1)}, bf16[128,1280]{1,0:T(8,128)(2,1)}, bf16[128,1280]{1,0:T(8,128)(2,1)}, bf16[320,2560]{1,0:T(8,128)(2,1)}) custom-call(s32[1,8]{1,0:T(1,128)} %seg_ref.1, bf16[128,1280]{1,0:T(8,128)(2,1)} %bitcast.9, bf16[128,1280]{1,0:T(8,128)(2,1)} %bitcast.10, ...), custom_call_target="tpu_custom_call" | custom-call | tf_op jit(solution)/shard_map/pallas_call | solution.py:636
  99.2 3.5 %shard_map.102 = (bf16[128,2560]{1,0:T(8,128)(2,1)}, bf16[128,1280]{1,0:T(8,128)(2,1)}, bf16[128,1280]{1,0:T(8,128)(2,1)}, bf16[128,1280]{1,0:T(8,128)(2,1)}, f32[320,2560]{1,0:T(8,128)}) custom-call(bf16[128,2560]{1,0:T(8,128)(2,1)} %get-tuple-element.15.refs_0_, bf16[128,1280]{1,0:T(8,128)(2,1)} %get-tuple-element.16.refs_1_, ...), custom_call_target="tpu_custom_call" | custom-call | tf_op jit(solution)/shard_map/pallas_call | solution.py:677

commit v5 on v4

--- a/solution.py
+++ b/solution.py
@@ -523,8 +523,8 @@
                 finish_inner(part - lag)
             for slot in range(slots):
                 send_some(slot, 1, range(part * n // parts, (part + 1) * n // parts))
-            if ndp == 4 and part >= parts - cuts:
-                partial_relay(order[part - parts + cuts])
+            if ndp == 4 and 3 <= part < 3 + cuts:
+                partial_relay(order[part - 3])
         for part in range(parts - lag, parts):
             finish_inner(part)
 
@@ -675,12 +675,12 @@
         ),
     )(seg_lengths, queries[0], keys[0], values[0], out_grad[0], w_out)
     attended, query_grad, key_grad, value_grad, weight_grad = pl.pallas_call(
-        functools.partial(copy_kernel, 5),
+        functools.partial(copy_kernel, 10),
         out_shape=out_shape,
         in_specs=anywhere,
         out_specs=tuple(anywhere),
         scratch_shapes=[pltpu.VMEM(x.shape, BF16) for x in out_shape]
-        + [pltpu.VMEM((wrows, width), F32), dma((13,)), dma((13,))],
+        + [pltpu.VMEM((wrows, width), F32), dma((18,)), dma((18,))],
         compiler_params=pltpu.CompilerParams(vmem_limit_bytes=VMEM_BYTES),
     )(*outputs)
     return (attended[None], query_grad[None], key_grad[None], value_grad[None], weight_grad)

time: 103 us -> 103 us (level)
  no operation moved by 1% of the time
where the time goes in v5:
time: 103 us
  Pallas kernels  102 us (99%)
    pallas_call x1, Pallas kernels, local(): pl.pallas_call(functools.partial(whole_kernel, n, ndp, parts, cuts, block...  98.6 us
    pallas_call x1, Pallas kernels, local(): pl.pallas_call(functools.partial(copy_kernel, 10), out_shape=out_shape, i...  3.47 us

profile of v5, /device:TPU:1, one launch (start us, length us, event | category | flops | bytes accessed | tf_op | source)
XLA Modules:
  0.0 102.7 jit_solution(1624932358627925789)
XLA Ops:
  0.6 98.6 %shard_map.101 = (bf16[128,2560]{1,0:T(8,128)(2,1)}, bf16[128,1280]{1,0:T(8,128)(2,1)}, bf16[128,1280]{1,0:T(8,128)(2,1)}, bf16[128,1280]{1,0:T(8,128)(2,1)}, bf16[320,2560]{1,0:T(8,128)(2,1)}) custom-call(s32[1,8]{1,0:T(1,128)} %seg_ref.1, bf16[128,1280]{1,0:T(8,128)(2,1)} %bitcast.9, bf16[128,1280]{1,0:T(8,128)(2,1)} %bitcast.10, ...), custom_call_target="tpu_custom_call" | custom-call | tf_op jit(solution)/shard_map/pallas_call | solution.py:636
  99.2 3.5 %shard_map.102 = (bf16[128,2560]{1,0:T(8,128)(2,1)}, bf16[128,1280]{1,0:T(8,128)(2,1)}, bf16[128,1280]{1,0:T(8,128)(2,1)}, bf16[128,1280]{1,0:T(8,128)(2,1)}, f32[320,2560]{1,0:T(8,128)}) custom-call(bf16[128,2560]{1,0:T(8,128)(2,1)} %get-tuple-element.15.refs_0_, bf16[128,1280]{1,0:T(8,128)(2,1)} %get-tuple-element.16.refs_1_, ...), custom_call_target="tpu_custom_call" | custom-call | tf_op jit(solution)/shard_map/pallas_call | solution.py:677
